TPU v7x, 512 devices: a whole 4x8x8 slice. The times are simulated.
512 devices in a mesh: tile: 64 (over x, y, core), fblk: 8 (over z).
Axes of the slice: x: 4, y: 8, z: 8, core: 2. Of those that a mesh axis runs over, the one named last changes fastest.
Arguments:
- planes: float32 [512, 1024, 128], P(('fblk', 'tile')), may hold values from -40000 to 40000
- widths: int32 [4], replicated, may hold values from 1 to 8, as said below
Outputs:
- peak_maps: float32 [4, 1024, 128], P(None, 'tile')
Inputs may be any that keep to these rules, and one draw needn't show every extreme that they name: `widths`: some kernel has width 8 in every draw.
All inputs are finite; a program needn't handle non-finite values.
Results may differ from a plain program's by a relative error of at most 0.0001.
Values sent between devices are 32-bit elements; how exact they have to be, the bound alone decides.
No kernel may reach another device: no remote copies, remote signals or barrier semaphores. Data moves between devices by JAX's collectives and lax.ppermute only.
A program may use at most 64 MiB of HBM per device.

v0:
```python
import jax
import jax.numpy as jnp
from jax import lax
from jax.sharding import PartitionSpec as P

KERNELS = 4
RAD = 8
MAXW = 8
SIGMAS = (1.0, 1.6, 2.3, 3.2)
EPSILON = 1e-06


def shifted(block, axis, distance):
    devices = range(lax.axis_size(axis))
    route = [(i - distance, i) for i in devices if i - distance in devices]
    return lax.ppermute(block, axis, route)


def with_halo(value, sides, width):
    for axis, dim in sides:
        peers, length = (lax.axis_size(axis), value.shape[dim])
        up = [(i, (i + 1) % peers) for i in range(peers - 1)]
        down = [(j, i) for i, j in up]
        last = lax.slice_in_dim(value, length - width, length, axis=dim)
        leading = lax.slice_in_dim(value, 0, width, axis=dim)
        before = lax.ppermute(last, axis, up)
        after = lax.ppermute(leading, axis, down)
        value = jnp.concatenate([before, value, after], axis=dim)
    return value


def kernel_for(sigma):
    offsets = jnp.arange(2 * RAD + 1).astype(jnp.float32) - RAD
    values = jnp.exp(-offsets * offsets / (2.0 * sigma * sigma))
    return values / jnp.sum(values)


def pad_along(values, along):
    margins = [(0, 0)] * values.ndim
    margins[along] = (RAD, RAD)
    return jnp.pad(values, margins)


def filter_along(padded, kernel, along):
    length = padded.shape[along] - 2 * RAD
    summed = jnp.zeros(lax.slice_in_dim(padded, 0, length, axis=along).shape, jnp.float32)
    for offset in range(2 * RAD + 1):
        summed = summed + kernel[offset] * lax.slice_in_dim(
            padded, offset, offset + length, axis=along
        )
    return summed


def boxcar(extended, width, channels):
    scale = 1.0 / jnp.sqrt(width.astype(jnp.float32))
    summed = jnp.zeros((channels,) + extended.shape[1:], jnp.float32)
    for offset in range(MAXW):
        weight = jnp.where(offset < width, 1.0, 0.0).astype(jnp.float32) * scale
        summed = summed + weight * extended[offset : offset + channels]
    return summed


def channel_peak(smoothed, sum_squares, cells):
    rms_values = jnp.sqrt(sum_squares / cells + EPSILON)
    return jnp.max(smoothed / rms_values[:, None, None], axis=0)


def body(planes, widths):
    relaid = lax.all_to_all(planes, "tile", split_axis=1, concat_axis=0, tiled=True)
    channels = relaid.shape[0]
    cells = relaid.shape[1] * lax.axis_size("tile") * relaid.shape[2]
    band_edge = shifted(relaid[: MAXW - 1], "fblk", -1)
    extended = jnp.concatenate([relaid, band_edge], axis=0)
    peak_list = []
    for kernel_id in range(KERNELS):
        kernel = kernel_for(SIGMAS[kernel_id])
        spectral = boxcar(extended, widths[kernel_id], channels)
        horizontal = filter_along(pad_along(spectral, 2), kernel, 2)
        bordered = with_halo(horizontal, (("tile", 1),), RAD)
        smoothed = filter_along(bordered, kernel, 1)
        sum_squares = lax.psum(jnp.sum(smoothed * smoothed, axis=(1, 2)), "tile")
        peak_list.append(channel_peak(smoothed, sum_squares, cells))
    return lax.pmax(jnp.stack(peak_list), "fblk")


def solution(mesh):
    placed = (P(("fblk", "tile"), None, None), P())
    return jax.shard_map(
        body, mesh=mesh, in_specs=placed, out_specs=P(None, "tile", None), check_vma=False
    )
```

profile of v0, /device:TPU:64, one launch (start us, length us, event | category | flops | bytes accessed | tf_op | source)
XLA Modules:
  0.0 334.0 jit_solution(15228907142696872255)
XLA Ops:
  0.0 0.0 copy-start
  0.0 10.7 %all-to-all-start = ((f32[1,1024,128]{2,0,1:T(1,128)}), f32[1,1024,128]{2,0,1:T(1,128)S(1)}, u32[]{:S(2)}, u32[]{:S(2)}) async-start(f32[1,1024,128]{2,0,1:T(1,128)} %bitcast.111), calls=%async_computation | async-start | bytes 1048576 | tf_op jit(solution)/shard_map/all_to_all | solution.py:69
  10.7 0.0 copy-done
  10.7 0.6 fusion.338
  34.4 0.6 fusion.321
  35.1 0.7 fusion.320
  35.7 0.6 fusion.319
  36.4 0.7 fusion.318
  37.1 0.6 broadcast_divide_fusion.3
  37.7 0.6 broadcast_divide_fusion.2
  38.3 0.6 broadcast_divide_fusion.1
  39.0 0.6 broadcast_divide_fusion
  39.6 0.7 fusion.340
  40.3 0.7 fusion.339
  41.1 0.7 fusion.337
  41.8 0.0 all-to-all-done
  41.8 1.9 collective-permute-start
  43.7 0.7 fusion.336
  44.4 3.8 %collective-permute-done = f32[7,16,128]{2,1,0:T(8,128)S(1)} collective-permute-done((f32[7,16,128]{2,1,0:T(8,128)S(1)}, f32[7,16,128]{2,1,0:T(8,128)S(1)}, u32[]{:S(2)}, u32[]{:S(2)}) %collective-permute-start) | collective-permute-done | bytes 57376 | tf_op jit(solution)/shard_map/ppermute | solution.py:16
  48.2 0.4 multiply_add_fusion.3
  48.6 0.3 multiply_add_fusion.2
  48.9 12.7 %fusion.230 = f32[64,16,128]{2,1,0:T(8,128)S(1)} fusion(f32[64,16,128]{2,1,0:T(8,128)S(1)} %multiply_add_fusion.2, f32[]{:T(128)} %bitcast.53, f32[]{:T(128)} %bitcast.52, f32[]{:T(128)} %bitcast.51, f32[]{:T(128)} %bitcast.50, f32[]{:T(128)} %bitcast.49, f32[]{:T(128)} %bitcast.48, f32[]{:T(128)} %bitcast.47, f32[]{:T(128)} %bitcast.46, f32[]{:T(128)} %bitcast.45, ...), kind=kLoop, calls=%fused_computation.418 | loop fusion | flops 4325376 | bytes 1048644 | tf_op jit(solution)/shard_map/add | solution.py:48
  61.6 1.3 collective-permute-start.3
  62.9 1.3 collective-permute-start.4
  64.2 0.3 multiply_add_fusion
  64.5 12.8 %fusion.294 = f32[64,16,128]{2,1,0:T(8,128)S(1)} fusion(f32[64,16,128]{2,1,0:T(8,128)S(1)} %multiply_add_fusion, f32[]{:T(128)} %bitcast.105, f32[]{:T(128)} %bitcast.104, f32[]{:T(128)} %bitcast.103, f32[]{:T(128)} %bitcast.102, f32[]{:T(128)} %bitcast.101, f32[]{:T(128)} %bitcast.100, f32[]{:T(128)} %bitcast.99, f32[]{:T(128)} %bitcast.98, f32[]{:T(128)} %bitcast.97, ...), kind=kLoop, calls=%fused_computation.482 | loop fusion | flops 4325376 | bytes 1048644 | tf_op jit(solution)/shard_map/add | solution.py:48
  77.3 4.9 %collective-permute-start.7 = (f32[64,8,128]{2,1,0:T(8,128)S(1)}, f32[64,8,128]{2,1,0:T(8,128)S(1)}, u32[]{:S(2)}, u32[]{:S(2)}) collective-permute-start(f32[64,8,128]{2,1,0:T(8,128)S(1)} %get-tuple-element.30), channel_id=1, source_target_pairs={{0,8},{8,16},{16,24},{24,32},{32,40},{40,48},{48,56},{56,64},{64,7... | collective-permute-start | bytes 786440 | tf_op jit(solution)/shard_map/ppermute | solution.py:26
  82.2 1.3 collective-permute-start.8
  83.5 0.3 multiply_add_fusion.1
  83.8 12.9 %fusion.262 = f32[64,16,128]{2,1,0:T(8,128)S(1)} fusion(f32[64,16,128]{2,1,0:T(8,128)S(1)} %multiply_add_fusion.1, f32[]{:T(128)} %bitcast.79, f32[]{:T(128)} %bitcast.78, f32[]{:T(128)} %bitcast.77, f32[]{:T(128)} %bitcast.76, f32[]{:T(128)} %bitcast.75, f32[]{:T(128)} %bitcast.74, f32[]{:T(128)} %bitcast.73, f32[]{:T(128)} %bitcast.72, f32[]{:T(128)} %bitcast.71, ...), kind=kLoop, calls=%fused_computation.450 | loop fusion | flops 4325376 | bytes 1048644 | tf_op jit(solution)/shard_map/add | solution.py:48
  96.8 4.3 %collective-permute-start.5 = (f32[64,8,128]{2,1,0:T(8,128)S(1)}, f32[64,8,128]{2,1,0:T(8,128)S(1)}, u32[]{:S(2)}, u32[]{:S(2)}) collective-permute-start(f32[64,8,128]{2,1,0:T(8,128)S(1)} %get-tuple-element.28), channel_id=1, source_target_pairs={{0,8},{8,16},{16,24},{24,32},{32,40},{40,48},{48,56},{56,64},{64,7... | collective-permute-start | bytes 786440 | tf_op jit(solution)/shard_map/ppermute | solution.py:26
  101.0 12.8 %fusion.198 = f32[64,16,128]{2,1,0:T(8,128)S(1)} fusion(f32[64,16,128]{2,1,0:T(8,128)S(1)} %get-tuple-element.11, f32[]{:T(128)} %bitcast.27, f32[]{:T(128)} %bitcast.26, f32[]{:T(128)} %bitcast.25, f32[]{:T(128)} %bitcast.24, f32[]{:T(128)} %bitcast.23, f32[]{:T(128)} %bitcast.22, f32[]{:T(128)} %bitcast.21, f32[]{:T(128)} %bitcast.20, f32[]{:T(128)} %bitcast.19, ...), kind=kLoop, calls=%fused_computation.386 | loop fusion | flops 4325376 | bytes 1048644 | tf_op jit(solution)/shard_map/add | solution.py:48
  113.9 0.0 collective-permute-done.3
  113.9 1.3 collective-permute-start.6
  115.2 0.0 collective-permute-done.4
  115.2 4.4 %collective-permute-start.1 = (f32[64,8,128]{2,1,0:T(8,128)S(1)}, f32[64,8,128]{2,1,0:T(8,128)S(1)}, u32[]{:S(2)}, u32[]{:S(2)}) collective-permute-start(f32[64,8,128]{2,1,0:T(8,128)S(1)} %get-tuple-element.24), channel_id=1, source_target_pairs={{0,8},{8,16},{16,24},{24,32},{32,40},{40,48},{48,56},{56,64},{64,7... | collective-permute-start | bytes 786440 | tf_op jit(solution)/shard_map/ppermute | solution.py:26
  119.7 12.5 %multiply_reduce_fusion.2 = (f32[64]{0:T(128)S(1)}, f32[64,16,128]{2,1,0:T(8,128)S(1)}) fusion(f32[64,8,128]{2,1,0:T(8,128)S(1)} %collective-permute-done.4, f32[64,16,128]{2,1,0:T(8,128)S(1)} %fusion.230, f32[]{:T(128)} %bitcast.53, f32[]{:T(128)} %bitcast.52, f32[]{:T(128)} %bitcast.51, f32[]{:T(128)} %bitcast.50, f32[]{:T(128)} %bitcast.49, f32[]{:T(128)} %bitcast.48, ...), kind=kLoop, calls=%fused_computation.519 | loop fusion | flops 6684608 | bytes 1573188 | tf_op jit(solution)/shard_map/reduce_sum | solution.py:81
  132.2 0.0 collective-permute-done.7
  132.2 1.3 collective-permute-start.2
  133.5 0.0 collective-permute-done.8
  133.5 12.6 %multiply_reduce_fusion = (f32[64]{0:T(128)S(1)}, f32[64,16,128]{2,1,0:T(8,128)S(1)}) fusion(f32[64,8,128]{2,1,0:T(8,128)S(1)} %collective-permute-done.8, f32[64,16,128]{2,1,0:T(8,128)S(1)} %fusion.294, f32[]{:T(128)} %bitcast.105, f32[]{:T(128)} %bitcast.104, f32[]{:T(128)} %bitcast.103, f32[]{:T(128)} %bitcast.102, f32[]{:T(128)} %bitcast.101, ...), kind=kLoop, calls=%fused_computation.515 | loop fusion | flops 6684608 | bytes 1573188 | tf_op jit(solution)/shard_map/reduce_sum | solution.py:81
  146.1 0.0 collective-permute-done.5
  146.1 0.0 collective-permute-done.6
  146.1 12.7 %multiply_reduce_fusion.1 = (f32[64]{0:T(128)S(1)}, f32[64,16,128]{2,1,0:T(8,128)S(1)}) fusion(f32[64,8,128]{2,1,0:T(8,128)S(1)} %collective-permute-done.6, f32[64,16,128]{2,1,0:T(8,128)S(1)} %fusion.262, f32[]{:T(128)} %bitcast.79, f32[]{:T(128)} %bitcast.78, f32[]{:T(128)} %bitcast.77, f32[]{:T(128)} %bitcast.76, f32[]{:T(128)} %bitcast.75, f32[]{:T(128)} %bitcast.74, ...), kind=kLoop, calls=%fused_computation.517 | loop fusion | flops 6684608 | bytes 1573188 | tf_op jit(solution)/shard_map/reduce_sum | solution.py:81
  158.8 0.0 collective-permute-done.1
  158.8 0.0 collective-permute-done.2
  158.8 12.6 %multiply_reduce_fusion.3 = (f32[64]{0:T(128)S(1)}, f32[64,16,128]{2,1,0:T(8,128)S(1)}) fusion(f32[64,8,128]{2,1,0:T(8,128)S(1)} %collective-permute-done.2, f32[64,16,128]{2,1,0:T(8,128)S(1)} %fusion.198, f32[]{:T(128)} %bitcast.27, f32[]{:T(128)} %bitcast.26, f32[]{:T(128)} %bitcast.25, f32[]{:T(128)} %bitcast.24, f32[]{:T(128)} %bitcast.23, f32[]{:T(128)} %bitcast.22, ...), kind=kLoop, calls=%fused_computation.521 | loop fusion | flops 6684608 | bytes 1573188 | tf_op jit(solution)/shard_map/reduce_sum | solution.py:81
  171.5 130.0 %all-reduce.4 = (f32[64]{0:T(128)S(1)}, f32[64]{0:T(128)S(1)}, f32[64]{0:T(128)S(1)}, f32[64]{0:T(128)S(1)}) all-reduce(f32[64]{0:T(128)S(1)} %get-tuple-element.22, f32[64]{0:T(128)S(1)} %get-tuple-element.20, f32[64]{0:T(128)S(1)} %get-tuple-element.18, f32[64]{0:T(128)S(1)} %get-tuple-element.9), channel_id=1, replica_groups=mesh['tile'=64,'fblk'=8] {'tile'}, use_global_device_ids=true, to_apply=%region_14.15 | all-reduce | flops 256 | bytes 2048 | tf_op jit(solution)/shard_map/psum | solution.py:81
  301.5 0.1 divide_reduce_fusion.1
  301.6 0.1 divide_reduce_fusion
  301.8 0.1 divide_reduce_fusion.3
  302.0 0.1 divide_reduce_fusion.2
  302.1 31.9 %pmax.7 = f32[4,16,128]{2,1,0:T(8,128)} all-reduce(f32[4,16,128]{2,1,0:T(8,128)S(1)} %pad_maximum_fusion.9), channel_id=1, replica_groups=mesh['tile'=64,'fblk'=8] {'fblk'}, use_global_device_ids=true, to_apply=%region_16.17 | all-reduce | flops 8192 | bytes 65536 | tf_op jit(solution)/shard_map/pmax | solution.py:83
  (8 shorter events, 0.2 us)
Async XLA Ops:
  0.0 10.7 %copy-start = (s32[4]{0:T(128)S(1)}, s32[4]{0:T(128)}, u32[]{:S(2)}) copy-start(s32[4]{0:T(128)} %param.3) | copy-start | bytes 52
  0.0 41.8 %all-to-all-start = ((f32[1,1024,128]{2,0,1:T(1,128)}), f32[1,1024,128]{2,0,1:T(1,128)S(1)}, u32[]{:S(2)}, u32[]{:S(2)}) async-start(f32[1,1024,128]{2,0,1:T(1,128)} %bitcast.111), calls=%async_computation | async-start | bytes 1048576 | tf_op jit(solution)/shard_map/all_to_all | solution.py:69
  41.8 6.4 %collective-permute-start = (f32[7,16,128]{2,1,0:T(8,128)S(1)}, f32[7,16,128]{2,1,0:T(8,128)S(1)}, u32[]{:S(2)}, u32[]{:S(2)}) collective-permute-start(f32[7,16,128]{2,1,0:T(8,128)S(1)} %bitcast.112), channel_id=1, source_target_pairs={{1,0},{2,1},{3,2},{4,3},{5,4},{6,5},{7,6},{9,8},{10,9},{11,10},{12... | collective-permute-start | bytes 172040 | tf_op jit(solution)/shard_map/ppermute | solution.py:16
  61.6 52.3 %collective-permute-start.3 = (f32[64,8,128]{2,1,0:T(8,128)S(1)}, f32[64,8,128]{2,1,0:T(8,128)S(1)}, u32[]{:S(2)}, u32[]{:S(2)}) collective-permute-start(f32[64,8,128]{2,1,0:T(8,128)S(1)} %get-tuple-element.26), channel_id=1, source_target_pairs={{0,8},{8,16},{16,24},{24,32},{32,40},{40,48},{48,56},{56,64},{64,7... | collective-permute-start | bytes 786440 | tf_op jit(solution)/shard_map/ppermute | solution.py:26
  62.9 52.3 %collective-permute-start.4 = (f32[64,8,128]{2,1,0:T(8,128)S(1)}, f32[64,8,128]{2,1,0:T(8,128)S(1)}, u32[]{:S(2)}, u32[]{:S(2)}) collective-permute-start(f32[64,8,128]{2,1,0:T(8,128)S(1)} %get-tuple-element.27), channel_id=1, source_target_pairs={{8,0},{16,8},{24,16},{32,24},{40,32},{48,40},{56,48},{64,56},{72,6... | collective-permute-start | bytes 786440 | tf_op jit(solution)/shard_map/ppermute | solution.py:27
  77.3 54.9 %collective-permute-start.7 = (f32[64,8,128]{2,1,0:T(8,128)S(1)}, f32[64,8,128]{2,1,0:T(8,128)S(1)}, u32[]{:S(2)}, u32[]{:S(2)}) collective-permute-start(f32[64,8,128]{2,1,0:T(8,128)S(1)} %get-tuple-element.30), channel_id=1, source_target_pairs={{0,8},{8,16},{16,24},{24,32},{32,40},{40,48},{48,56},{56,64},{64,7... | collective-permute-start | bytes 786440 | tf_op jit(solution)/shard_map/ppermute | solution.py:26
  82.2 51.3 %collective-permute-start.8 = (f32[64,8,128]{2,1,0:T(8,128)S(1)}, f32[64,8,128]{2,1,0:T(8,128)S(1)}, u32[]{:S(2)}, u32[]{:S(2)}) collective-permute-start(f32[64,8,128]{2,1,0:T(8,128)S(1)} %get-tuple-element.31), channel_id=1, source_target_pairs={{8,0},{16,8},{24,16},{32,24},{40,32},{48,40},{56,48},{64,56},{72,6... | collective-permute-start | bytes 786440 | tf_op jit(solution)/shard_map/ppermute | solution.py:27
  96.8 49.3 %collective-permute-start.5 = (f32[64,8,128]{2,1,0:T(8,128)S(1)}, f32[64,8,128]{2,1,0:T(8,128)S(1)}, u32[]{:S(2)}, u32[]{:S(2)}) collective-permute-start(f32[64,8,128]{2,1,0:T(8,128)S(1)} %get-tuple-element.28), channel_id=1, source_target_pairs={{0,8},{8,16},{16,24},{24,32},{32,40},{40,48},{48,56},{56,64},{64,7... | collective-permute-start | bytes 786440 | tf_op jit(solution)/shard_map/ppermute | solution.py:26
  113.9 32.2 %collective-permute-start.6 = (f32[64,8,128]{2,1,0:T(8,128)S(1)}, f32[64,8,128]{2,1,0:T(8,128)S(1)}, u32[]{:S(2)}, u32[]{:S(2)}) collective-permute-start(f32[64,8,128]{2,1,0:T(8,128)S(1)} %get-tuple-element.29), channel_id=1, source_target_pairs={{8,0},{16,8},{24,16},{32,24},{40,32},{48,40},{56,48},{64,56},{72,6... | collective-permute-start | bytes 786440 | tf_op jit(solution)/shard_map/ppermute | solution.py:27
  115.2 43.6 %collective-permute-start.1 = (f32[64,8,128]{2,1,0:T(8,128)S(1)}, f32[64,8,128]{2,1,0:T(8,128)S(1)}, u32[]{:S(2)}, u32[]{:S(2)}) collective-permute-start(f32[64,8,128]{2,1,0:T(8,128)S(1)} %get-tuple-element.24), channel_id=1, source_target_pairs={{0,8},{8,16},{16,24},{24,32},{32,40},{40,48},{48,56},{56,64},{64,7... | collective-permute-start | bytes 786440 | tf_op jit(solution)/shard_map/ppermute | solution.py:26
  132.2 26.6 %collective-permute-start.2 = (f32[64,8,128]{2,1,0:T(8,128)S(1)}, f32[64,8,128]{2,1,0:T(8,128)S(1)}, u32[]{:S(2)}, u32[]{:S(2)}) collective-permute-start(f32[64,8,128]{2,1,0:T(8,128)S(1)} %get-tuple-element.25), channel_id=1, source_target_pairs={{8,0},{16,8},{24,16},{32,24},{40,32},{48,40},{56,48},{64,56},{72,6... | collective-permute-start | bytes 786440 | tf_op jit(solution)/shard_map/ppermute | solution.py:27
where the time goes:
time: 336 us; the launch traced here: 334 us
  blocking collectives  162 us (48%)
  other arithmetic  109 us (32%)
  starting transfers between devices  32.7 us (10%)
  between operations  23.4 us (7%)
  waiting for transfers between devices  3.8 us (1%)
  local copies, waits for them, and re-layouts  3.62 us (1%)
    psum x1, blocking collectives, body(): sum_squares = lax.psum(jnp.sum(smoothed * smoothed, axis=(1, 2)), 'tile')  130 us
    add x4, other arithmetic, filter_along(): summed + kernel[offset] * lax.slice_in_dim(padded, offset, offset + lengt...  51.2 us
    reduce_sum x4, other arithmetic, body(): sum_squares = lax.psum(jnp.sum(smoothed * smoothed, axis=(1, 2)), 'tile')  50.4 us
    pmax x1, blocking collectives, body(): return lax.pmax(jnp.stack(peak_list), 'fblk')  31.9 us
    ppermute x4, starting transfers between devices, with_halo(): before = lax.ppermute(last, axis, up)  14.9 us
    all_to_all x1, starting transfers between devices, body(): lax.all_to_all(planes, 'tile', split_axis=1, concat_axis=0, tiled=True)  10.7 us
  transfers between devices with their start and end apart: 10, of which 1 were waited for; matrix products, arithmetic and copies ran while one was open for 26% of the time, Pallas kernels for 0%

commit v1 on v0

--- a/solution.py
+++ b/solution.py
@@ -78,7 +78,9 @@
         horizontal = filter_along(pad_along(spectral, 2), kernel, 2)
         bordered = with_halo(horizontal, (("tile", 1),), RAD)
         smoothed = filter_along(bordered, kernel, 1)
-        sum_squares = lax.psum(jnp.sum(smoothed * smoothed, axis=(1, 2)), "tile")
+        own = jnp.sum(smoothed * smoothed, axis=(1, 2))
+        parts = lax.all_gather(own, "tile", axis=0, tiled=False)
+        sum_squares = parts.sum(axis=0)
         peak_list.append(channel_peak(smoothed, sum_squares, cells))
     return lax.pmax(jnp.stack(peak_list), "fblk")
 

time: 336 us -> 426 us (1.27)
  the two profiles are of different devices: /device:TPU:64 before, /device:TPU:2 now
where the time goes in v1:
time: 426 us; the launch traced here: 424 us
  waiting for transfers between devices  184 us (43%)
  other arithmetic  115 us (27%)
  starting transfers between devices  42.8 us (10%)
  between operations  37.4 us (9%)
  blocking collectives  31.5 us (7%)
  local copies, waits for them, and re-layouts  12.6 us (3%)
    unnamed x2, waiting for transfers between devices  180 us
    reduce_sum x4, other arithmetic, body(): own = jnp.sum(smoothed * smoothed, axis=(1, 2))  56.8 us
    add x4, other arithmetic, filter_along(): summed + kernel[offset] * lax.slice_in_dim(padded, offset, offset + lengt...  51.3 us
    pmax x1, blocking collectives, body(): return lax.pmax(jnp.stack(peak_list), 'fblk')  31.5 us
    ppermute x4, starting transfers between devices, with_halo(): after = lax.ppermute(leading, axis, down)  23 us
    all_to_all x1, starting transfers between devices, body(): lax.all_to_all(planes, 'tile', split_axis=1, concat_axis=0, tiled=True)  10.7 us
  transfers between devices with their start and end apart: 11, of which 2 were waited for; matrix products, arithmetic and copies ran while one was open for 22% of the time, Pallas kernels for 0%

profile of v1, /device:TPU:2, one launch (start us, length us, event | category | flops | bytes accessed | tf_op | source)
XLA Modules:
  0.0 423.6 jit_solution(8029322721546994997)
XLA Ops:
  6.5 10.7 %all-to-all-start = ((f32[1,1024,128]{2,0,1:T(1,128)}), f32[1,1024,128]{2,0,1:T(1,128)S(1)}, u32[]{:S(2)}, u32[]{:S(2)}) async-start(f32[1,1024,128]{2,0,1:T(1,128)} %bitcast.112), calls=%async_computation | async-start | bytes 1048576 | tf_op jit(solution)/shard_map/all_to_all | solution.py:69
  17.2 0.0 all-reduce.11.cloned.1.call-start
  17.3 0.0 copy-start.8
  17.3 0.6 copy-done.8
  17.9 0.6 fusion.338
  41.6 1.3 dynamic-slice
  43.5 0.6 fusion.321
  44.1 0.7 fusion.320
  44.8 0.6 fusion.319
  45.4 0.7 fusion.318
  46.1 0.6 broadcast_divide_fusion.3
  46.7 0.6 broadcast_divide_fusion.2
  47.3 0.7 broadcast_divide_fusion.1
  48.0 0.6 broadcast_divide_fusion
  48.7 0.7 fusion.340
  49.4 0.7 fusion.339
  50.1 0.7 fusion.337
  50.8 0.0 all-to-all-done
  50.8 1.3 collective-permute-start
  52.1 0.7 fusion.336
  52.8 4.5 %collective-permute-done = f32[7,16,128]{2,1,0:T(8,128)S(1)} collective-permute-done((f32[7,16,128]{2,1,0:T(8,128)S(1)}, f32[7,16,128]{2,1,0:T(8,128)S(1)}, u32[]{:S(2)}, u32[]{:S(2)}) %collective-permute-start) | collective-permute-done | bytes 57376 | tf_op jit(solution)/shard_map/ppermute | solution.py:16
  57.3 0.4 multiply_add_fusion.3
  57.7 0.3 multiply_add_fusion.2
  58.0 12.8 %fusion.230 = f32[64,16,128]{2,1,0:T(8,128)S(1)} fusion(f32[64,16,128]{2,1,0:T(8,128)S(1)} %multiply_add_fusion.2, f32[]{:T(128)} %bitcast.54, f32[]{:T(128)} %bitcast.53, f32[]{:T(128)} %bitcast.52, f32[]{:T(128)} %bitcast.51, f32[]{:T(128)} %bitcast.50, f32[]{:T(128)} %bitcast.49, f32[]{:T(128)} %bitcast.48, f32[]{:T(128)} %bitcast.47, f32[]{:T(128)} %bitcast.46, ...), kind=kLoop, calls=%fused_computation.418 | loop fusion | flops 4325376 | bytes 1048644 | tf_op jit(solution)/shard_map/add | solution.py:48
  70.8 1.9 collective-permute-start.3
  72.8 5.8 %collective-permute-start.4 = (f32[64,8,128]{2,1,0:T(8,128)S(1)}, f32[64,8,128]{2,1,0:T(8,128)S(1)}, u32[]{:S(2)}, u32[]{:S(2)}) collective-permute-start(f32[64,8,128]{2,1,0:T(8,128)S(1)} %get-tuple-element.27), channel_id=1, source_target_pairs={{8,0},{16,8},{24,16},{32,24},{40,32},{48,40},{56,48},{64,56},{72,6... | collective-permute-start | bytes 786440 | tf_op jit(solution)/shard_map/ppermute | solution.py:27
  78.5 0.3 multiply_add_fusion
  78.8 12.8 %fusion.294 = f32[64,16,128]{2,1,0:T(8,128)S(1)} fusion(f32[64,16,128]{2,1,0:T(8,128)S(1)} %multiply_add_fusion, f32[]{:T(128)} %bitcast.106, f32[]{:T(128)} %bitcast.105, f32[]{:T(128)} %bitcast.104, f32[]{:T(128)} %bitcast.103, f32[]{:T(128)} %bitcast.102, f32[]{:T(128)} %bitcast.101, f32[]{:T(128)} %bitcast.100, f32[]{:T(128)} %bitcast.99, f32[]{:T(128)} %bitcast.98, ...), kind=kLoop, calls=%fused_computation.482 | loop fusion | flops 4325376 | bytes 1048644 | tf_op jit(solution)/shard_map/add | solution.py:48
  91.6 0.8 fusion.335
  92.5 1.9 collective-permute-start.7
  94.4 5.8 %collective-permute-start.8 = (f32[64,8,128]{2,1,0:T(8,128)}, f32[64,8,128]{2,1,0:T(8,128)}, u32[]{:S(2)}, u32[]{:S(2)}) collective-permute-start(f32[64,8,128]{2,1,0:T(8,128)} %get-tuple-element.31), channel_id=1, source_target_pairs={{8,0},{16,8},{24,16},{32,24},{40,32},{48,40},{56,48},{64,56},{72,6... | collective-permute-start | bytes 786440 | tf_op jit(solution)/shard_map/ppermute | solution.py:27
  100.1 0.3 multiply_add_fusion.1
  100.4 12.7 %fusion.262 = f32[64,16,128]{2,1,0:T(8,128)S(1)} fusion(f32[64,16,128]{2,1,0:T(8,128)S(1)} %multiply_add_fusion.1, f32[]{:T(128)} %bitcast.80, f32[]{:T(128)} %bitcast.79, f32[]{:T(128)} %bitcast.78, f32[]{:T(128)} %bitcast.77, f32[]{:T(128)} %bitcast.76, f32[]{:T(128)} %bitcast.75, f32[]{:T(128)} %bitcast.74, f32[]{:T(128)} %bitcast.73, f32[]{:T(128)} %bitcast.72, ...), kind=kLoop, calls=%fused_computation.450 | loop fusion | flops 4325376 | bytes 1048644 | tf_op jit(solution)/shard_map/add | solution.py:48
  113.1 0.9 fusion.334
  114.0 1.9 collective-permute-start.5
  115.9 12.9 %fusion.198 = f32[64,16,128]{2,1,0:T(8,128)S(1)} fusion(f32[64,16,128]{2,1,0:T(8,128)S(1)} %get-tuple-element.11, f32[]{:T(128)} %bitcast.27, f32[]{:T(128)} %bitcast.26, f32[]{:T(128)} %bitcast.25, f32[]{:T(128)} %bitcast.24, f32[]{:T(128)} %bitcast.23, f32[]{:T(128)} %bitcast.22, f32[]{:T(128)} %bitcast.21, f32[]{:T(128)} %bitcast.20, f32[]{:T(128)} %bitcast.19, ...), kind=kLoop, calls=%fused_computation.386 | loop fusion | flops 4325376 | bytes 1048644 | tf_op jit(solution)/shard_map/add | solution.py:48
  128.8 0.7 fusion.332
  129.5 0.0 collective-permute-done.3
  129.6 5.7 %collective-permute-start.6 = (f32[64,8,128]{2,1,0:T(8,128)}, f32[64,8,128]{2,1,0:T(8,128)}, u32[]{:S(2)}, u32[]{:S(2)}) collective-permute-start(f32[64,8,128]{2,1,0:T(8,128)} %get-tuple-element.29), channel_id=1, source_target_pairs={{8,0},{16,8},{24,16},{32,24},{40,32},{48,40},{56,48},{64,56},{72,6... | collective-permute-start | bytes 786440 | tf_op jit(solution)/shard_map/ppermute | solution.py:27
  135.3 2.1 collective-permute-start.1
  137.4 12.6 %multiply_reduce_fusion.2 = (f32[64]{0:T(128)S(1)}, f32[64,16,128]{2,1,0:T(8,128)S(1)}) fusion(f32[64,8,128]{2,1,0:T(8,128)S(1)} %collective-permute-done.4, f32[64,16,128]{2,1,0:T(8,128)S(1)} %fusion.230, f32[]{:T(128)} %bitcast.54, f32[]{:T(128)} %bitcast.53, f32[]{:T(128)} %bitcast.52, f32[]{:T(128)} %bitcast.51, f32[]{:T(128)} %bitcast.50, f32[]{:T(128)} %bitcast.49, ...), kind=kLoop, calls=%fused_computation.519 | loop fusion | flops 6684608 | bytes 1573188 | tf_op jit(solution)/shard_map/reduce_sum | solution.py:81
  150.1 0.3 dynamic-update-slice.1
  150.3 5.8 %collective-permute-start.2 = (f32[64,8,128]{2,1,0:T(8,128)S(1)}, f32[64,8,128]{2,1,0:T(8,128)}, u32[]{:S(2)}, u32[]{:S(2)}) collective-permute-start(f32[64,8,128]{2,1,0:T(8,128)S(1)} %get-tuple-element.25), channel_id=1, source_target_pairs={{8,0},{16,8},{24,16},{32,24},{40,32},{48,40},{56,48},{64,56},{72,6... | collective-permute-start | bytes 786440 | tf_op jit(solution)/shard_map/ppermute | solution.py:27
  156.1 15.3 %multiply_reduce_fusion = (f32[64]{0:T(128)S(1)}, f32[64,16,128]{2,1,0:T(8,128)S(1)}) fusion(f32[64,8,128]{2,1,0:T(8,128)} %collective-permute-done.8, f32[64,16,128]{2,1,0:T(8,128)S(1)} %fusion.294, f32[]{:T(128)} %bitcast.106, f32[]{:T(128)} %bitcast.105, f32[]{:T(128)} %bitcast.104, f32[]{:T(128)} %bitcast.103, f32[]{:T(128)} %bitcast.102, f32[]{:T(128)} %bitcast.101, ...), kind=kLoop, calls=%fused_computation.515 | loop fusion | flops 6684608 | bytes 1573188 | tf_op jit(solution)/shard_map/reduce_sum | solution.py:81
  171.4 0.3 dynamic-update-slice.3
  171.7 14.3 %multiply_reduce_fusion.1 = (f32[64]{0:T(128)S(1)}, f32[64,16,128]{2,1,0:T(8,128)S(1)}) fusion(f32[64,8,128]{2,1,0:T(8,128)} %collective-permute-done.6, f32[64,16,128]{2,1,0:T(8,128)S(1)} %fusion.262, f32[]{:T(128)} %bitcast.80, f32[]{:T(128)} %bitcast.79, f32[]{:T(128)} %bitcast.78, f32[]{:T(128)} %bitcast.77, f32[]{:T(128)} %bitcast.76, f32[]{:T(128)} %bitcast.75, ...), kind=kLoop, calls=%fused_computation.517 | loop fusion | flops 6684608 | bytes 1573188 | tf_op jit(solution)/shard_map/reduce_sum | solution.py:81
  186.1 0.3 dynamic-update-slice.2
  186.3 14.6 %multiply_reduce_fusion.3 = (f32[64]{0:T(128)S(1)}, f32[64,16,128]{2,1,0:T(8,128)S(1)}) fusion(f32[64,8,128]{2,1,0:T(8,128)} %collective-permute-done.2, f32[64,16,128]{2,1,0:T(8,128)S(1)} %fusion.198, f32[]{:T(128)} %bitcast.27, f32[]{:T(128)} %bitcast.26, f32[]{:T(128)} %bitcast.25, f32[]{:T(128)} %bitcast.24, f32[]{:T(128)} %bitcast.23, f32[]{:T(128)} %bitcast.22, ...), kind=kLoop, calls=%fused_computation.521 | loop fusion | flops 6684608 | bytes 1573188 | tf_op jit(solution)/shard_map/reduce_sum | solution.py:81
  201.0 0.3 dynamic-update-slice
  201.3 0.6 copy-done.1
  201.9 0.0 all-reduce.11.cloned.1.call-update
  201.9 179.6 %all-reduce.11.cloned.1.call-done = (f32[4096]{0:T(1024)}, f32[4096]{0:T(1024)}, f32[4096]{0:T(1024)}, f32[4096]{0:T(1024)}) async-done(((f32[4096]{0:T(1024)}, f32[4096]{0:T(1024)}, f32[4096]{0:T(1024)}, f32[4096]{0:T(1024)}), (f32[4096]{0:T(1024)}, f32[4096]{0:T(1024)}, f32[4096]{0:T(1024)}, f32[4096]{0:T(1024)})) %all-reduce.11.cloned.1.call-update) | async-done | bytes 65552
  381.5 0.8 reshape.227
  382.3 0.7 copy-done.7
  383.0 0.1 reshape.226
  383.1 0.7 copy-done.6
  383.8 0.1 reshape.225
  383.9 0.7 copy-done.5
  384.6 0.1 reshape.224
  384.7 0.1 divide_reduce_fusion
  384.8 0.1 divide_reduce_fusion.1
  385.0 0.1 divide_reduce_fusion.2
  385.1 0.1 divide_reduce_fusion.3
  385.3 31.5 %pmax.7 = f32[4,16,128]{2,1,0:T(8,128)} all-reduce(f32[4,16,128]{2,1,0:T(8,128)S(1)} %pad_maximum_fusion.9), channel_id=1, replica_groups=mesh['tile'=64,'fblk'=8] {'fblk'}, use_global_device_ids=true, to_apply=%region_16.17 | all-reduce | flops 8192 | bytes 65536 | tf_op jit(solution)/shard_map/pmax | solution.py:85
  (34 shorter events, 0.2 us)
Async XLA Ops:
  6.5 44.3 %all-to-all-start = ((f32[1,1024,128]{2,0,1:T(1,128)}), f32[1,1024,128]{2,0,1:T(1,128)S(1)}, u32[]{:S(2)}, u32[]{:S(2)}) async-start(f32[1,1024,128]{2,0,1:T(1,128)} %bitcast.112), calls=%async_computation | async-start | bytes 1048576 | tf_op jit(solution)/shard_map/all_to_all | solution.py:69
  17.2 364.3 %all-reduce.11.cloned.1.call-start = ((), (), s32[]{:S(2)}) async-start(), calls=%async_computation.1 | async-start | bytes 131072
  17.3 0.7 copy-start.8
  50.8 6.5 %collective-permute-start = (f32[7,16,128]{2,1,0:T(8,128)S(1)}, f32[7,16,128]{2,1,0:T(8,128)S(1)}, u32[]{:S(2)}, u32[]{:S(2)}) collective-permute-start(f32[7,16,128]{2,1,0:T(8,128)S(1)} %bitcast.113), channel_id=1, source_target_pairs={{1,0},{2,1},{3,2},{4,3},{5,4},{6,5},{7,6},{9,8},{10,9},{11,10},{12... | collective-permute-start | bytes 172040 | tf_op jit(solution)/shard_map/ppermute | solution.py:16
  70.8 58.7 %collective-permute-start.3 = (f32[64,8,128]{2,1,0:T(8,128)S(1)}, f32[64,8,128]{2,1,0:T(8,128)S(1)}, u32[]{:S(2)}, u32[]{:S(2)}) collective-permute-start(f32[64,8,128]{2,1,0:T(8,128)S(1)} %get-tuple-element.26), channel_id=1, source_target_pairs={{0,8},{8,16},{16,24},{24,32},{32,40},{40,48},{48,56},{56,64},{64,7... | collective-permute-start | bytes 786440 | tf_op jit(solution)/shard_map/ppermute | solution.py:26
  72.8 62.5 %collective-permute-start.4 = (f32[64,8,128]{2,1,0:T(8,128)S(1)}, f32[64,8,128]{2,1,0:T(8,128)S(1)}, u32[]{:S(2)}, u32[]{:S(2)}) collective-permute-start(f32[64,8,128]{2,1,0:T(8,128)S(1)} %get-tuple-element.27), channel_id=1, source_target_pairs={{8,0},{16,8},{24,16},{32,24},{40,32},{48,40},{56,48},{64,56},{72,6... | collective-permute-start | bytes 786440 | tf_op jit(solution)/shard_map/ppermute | solution.py:27
  92.5 57.9 %collective-permute-start.7 = (f32[64,8,128]{2,1,0:T(8,128)}, f32[64,8,128]{2,1,0:T(8,128)S(1)}, u32[]{:S(2)}, u32[]{:S(2)}) collective-permute-start(f32[64,8,128]{2,1,0:T(8,128)} %get-tuple-element.30), channel_id=1, source_target_pairs={{0,8},{8,16},{16,24},{24,32},{32,40},{40,48},{48,56},{56,64},{64,7... | collective-permute-start | bytes 786440 | tf_op jit(solution)/shard_map/ppermute | solution.py:26
  94.4 61.7 %collective-permute-start.8 = (f32[64,8,128]{2,1,0:T(8,128)}, f32[64,8,128]{2,1,0:T(8,128)}, u32[]{:S(2)}, u32[]{:S(2)}) collective-permute-start(f32[64,8,128]{2,1,0:T(8,128)} %get-tuple-element.31), channel_id=1, source_target_pairs={{8,0},{16,8},{24,16},{32,24},{40,32},{48,40},{56,48},{64,56},{72,6... | collective-permute-start | bytes 786440 | tf_op jit(solution)/shard_map/ppermute | solution.py:27
  114.0 57.7 %collective-permute-start.5 = (f32[64,8,128]{2,1,0:T(8,128)}, f32[64,8,128]{2,1,0:T(8,128)S(1)}, u32[]{:S(2)}, u32[]{:S(2)}) collective-permute-start(f32[64,8,128]{2,1,0:T(8,128)} %get-tuple-element.28), channel_id=1, source_target_pairs={{0,8},{8,16},{16,24},{24,32},{32,40},{40,48},{48,56},{56,64},{64,7... | collective-permute-start | bytes 786440 | tf_op jit(solution)/shard_map/ppermute | solution.py:26
  129.6 42.2 %collective-permute-start.6 = (f32[64,8,128]{2,1,0:T(8,128)}, f32[64,8,128]{2,1,0:T(8,128)}, u32[]{:S(2)}, u32[]{:S(2)}) collective-permute-start(f32[64,8,128]{2,1,0:T(8,128)} %get-tuple-element.29), channel_id=1, source_target_pairs={{8,0},{16,8},{24,16},{32,24},{40,32},{48,40},{56,48},{64,56},{72,6... | collective-permute-start | bytes 786440 | tf_op jit(solution)/shard_map/ppermute | solution.py:27
  135.3 51.0 %collective-permute-start.1 = (f32[64,8,128]{2,1,0:T(8,128)}, f32[64,8,128]{2,1,0:T(8,128)S(1)}, u32[]{:S(2)}, u32[]{:S(2)}) collective-permute-start(f32[64,8,128]{2,1,0:T(8,128)} %get-tuple-element.24), channel_id=1, source_target_pairs={{0,8},{8,16},{16,24},{24,32},{32,40},{40,48},{48,56},{56,64},{64,7... | collective-permute-start | bytes 786440 | tf_op jit(solution)/shard_map/ppermute | solution.py:26
  150.3 21.1 %copy-start.2 = (f32[4096]{0:T(1024)}, f32[4096]{0:T(1024)S(1)}, u32[]{:S(2)}) copy-start(f32[4096]{0:T(1024)S(1)} %dynamic-update-slice.1) | copy-start | bytes 49156
  150.3 5.8 %copy-start = (f32[64,8,128]{2,1,0:T(8,128)}, f32[64,8,128]{2,1,0:T(8,128)S(1)}, u32[]{:S(2)}) copy-start(f32[64,8,128]{2,1,0:T(8,128)S(1)} %collective-permute-done.7) | copy-start | bytes 786436
  150.3 36.0 %collective-permute-start.2 = (f32[64,8,128]{2,1,0:T(8,128)S(1)}, f32[64,8,128]{2,1,0:T(8,128)}, u32[]{:S(2)}, u32[]{:S(2)}) collective-permute-start(f32[64,8,128]{2,1,0:T(8,128)S(1)} %get-tuple-element.25), channel_id=1, source_target_pairs={{8,0},{16,8},{24,16},{32,24},{40,32},{48,40},{56,48},{64,56},{72,6... | collective-permute-start | bytes 786440 | tf_op jit(solution)/shard_map/ppermute | solution.py:27
  171.7 14.3 %copy-start.3 = (f32[4096]{0:T(1024)}, f32[4096]{0:T(1024)S(1)}, u32[]{:S(2)}) copy-start(f32[4096]{0:T(1024)S(1)} %dynamic-update-slice.3) | copy-start | bytes 49156
  186.3 14.6 %copy-start.4 = (f32[4096]{0:T(1024)}, f32[4096]{0:T(1024)S(1)}, u32[]{:S(2)}) copy-start(f32[4096]{0:T(1024)S(1)} %dynamic-update-slice.2) | copy-start | bytes 49156
  201.3 0.6 copy-start.1
  382.3 0.7 copy-start.7
  383.1 0.7 copy-start.6
  383.9 0.7 copy-start.5
Sparse Core Ops, SparseCore 0:
  202.0 179.4 all-reduce.10
